TPU v7x, 32 devices: a whole 2x2x4 slice. The times are simulated.
32 devices in a mesh: scene: 2 (over x), az: 8 (over z, y), rg: 2 (over core).
Axes of the slice: x: 2, y: 2, z: 4, core: 2. Of those that a mesh axis runs over, the one named last changes fastest.
Arguments:
- complex_phase_image: float32 [2, 1024, 1024], P(None, ('scene', 'az'), 'rg'), parts along dimension 1, may hold values from -6 to 6
- phase_to_topography_factor: float32 [1024, 1024], P(('scene', 'az'), 'rg'), parts along dimension 0, may hold values from 0.5 to 3
- terrain_model_heights: float32 [128, 16, 1024], P(('scene', 'az'), 'rg'), parts along dimension 0, may hold values from -6 to 6
- radar_parcel_listing: int32 [32, 9], P(('scene', 'az', 'rg')), parts along dimension 0, may hold values from -1 to 1023, as said below
- pixel_terrain_position: int32 [1024, 1024], P(('scene', 'az'), 'rg'), parts along dimension 0, may hold values from 0 to 9215, as said below
- multilook_receiving_patch: int32 [65536, 1], P(('scene', 'az', 'rg')), parts along dimension 0, may hold values from 0 to 15; in each aligned block of 2048 rows (0 to 2047, 2048 to 4095, ...) at most 256 rows name the same one
- multilook_base_point: int32 [65536], P(('scene', 'az', 'rg')), parts along dimension 0, may hold values from 0 to 2047
- multilook_splat_shares: float32 [4, 65536], P(None, ('scene', 'az', 'rg')), parts along dimension 1, may hold values from 0 to 1
Outputs:
- geocoded: float32 [2, 256, 256], P(None, ('scene', 'az'), 'rg'), parts along dimension 1
There are 2 independent parts, one for each index of `scene`. A program takes and returns all parts, laid end to end along the dimension named above; each array names one. Nothing has to cross between parts.
Inputs may be any that keep to these rules, and one draw needn't show every extreme that they name: `radar_parcel_listing`: entries are sub-block numbers lat * 16 + lon; each tile lists a rectangle of at most 3 x 3 sub-blocks in row-major order, then -1 padding. Tile (a, r) lists only sub-blocks with c * 8 - 1 <= lat <= (c + 1) * 8 for one map latitude row c (any row, not tied to a) and r * 8 - 1 <= lon <= (r + 1) * 8. Some tile has exactly 9 listed blocks. pixel_terrain_position // 1024 is a listed, non-padding slot of the pixel's own tile. `multilook_receiving_patch`: among the rows of one device (aligned blocks of 2048 rows) at most 256 name one map tile; some map tile is named by exactly 256 rows of some device.
All inputs are finite; a program needn't handle non-finite values.
Results may differ from a plain program's by a relative error of at most 0.00015.
Values sent between devices are 32-bit elements; how exact they have to be, the bound alone decides.
A program may use at most 64 MiB of HBM per device.

v0:
```python
import functools
import math

import jax
import jax.numpy as jnp
import numpy as np
from jax import lax
from jax.experimental import pallas as pl
from jax.experimental.pallas import tpu as pltpu
from jax.sharding import PartitionSpec as P

PATCH = 64
LOOK = 4
LANES = 128
EPS = 1e-06
F32 = jnp.float32
BF16 = jnp.bfloat16


def halves(value):
    high = value.astype(BF16)
    return high, (value - high.astype(F32)).astype(BF16)


def filter_tables():
    steps = np.arange(PATCH)
    angle = (steps[:, None] * steps[None, :] % PATCH) * (2.0 * math.pi / PATCH)
    cosine, sine = np.cos(angle), np.sin(angle)
    left = np.block([[cosine, sine], [-sine, cosine]])
    step, wide = PATCH // 2, 4 * PATCH
    right = np.zeros((2 * wide, 2 * wide))
    for p in range(4):
        rows, cols = slice(p * step, p * step + PATCH), slice(p * PATCH, (p + 1) * PATCH)
        rows_im = slice(wide + p * step, wide + p * step + PATCH)
        cols_im = slice(wide + p * PATCH, wide + (p + 1) * PATCH)
        right[rows, cols] = cosine
        right[rows, cols_im] = -sine
        right[rows_im, cols] = sine
        right[rows_im, cols_im] = cosine
    group = np.arange(wide) // PATCH
    same = group[:, None] == group[None, :]
    gap = (np.arange(wide)[:, None] - np.arange(wide)[None, :]) % PATCH
    band = same & ((gap <= 1) | (gap == PATCH - 1))
    cells = PATCH // 2 // LOOK
    places = PATCH // 4 + np.arange(cells * LOOK)
    turn = steps[:, None] * places[None, :] % PATCH * (2.0 * math.pi / PATCH)
    mean_re = np.cos(turn).reshape(PATCH, cells, LOOK).mean(axis=2) / PATCH
    mean_im = np.sin(turn).reshape(PATCH, cells, LOOK).mean(axis=2) / PATCH
    back_left = np.block([[mean_re.T, -mean_im.T], [mean_im.T, mean_re.T]])
    back_right = np.zeros((2 * wide, 8 * cells))
    for p in range(4):
        rows = slice(p * PATCH, (p + 1) * PATCH)
        rows_im = slice(wide + p * PATCH, wide + (p + 1) * PATCH)
        cols = slice(p * cells, (p + 1) * cells)
        cols_im = slice((4 + p) * cells, (5 + p) * cells)
        back_right[rows, cols] = mean_re
        back_right[rows, cols_im] = mean_im
        back_right[rows_im, cols] = -mean_im
        back_right[rows_im, cols_im] = mean_re
    tables = []
    for table in (left, right, back_left, back_right):
        high = table.astype(np.float32).astype(jnp.bfloat16)
        tables += [high, (table - high.astype(np.float64)).astype(jnp.bfloat16)]
    return tables + [band.astype(jnp.bfloat16), same.astype(jnp.bfloat16)]


def sine_cosine(angle):
    turns = jnp.floor(angle * (2.0 / math.pi) + 0.5)
    rest = angle - turns * 1.5703125
    rest = rest - turns * 4.837512969970703e-04
    rest = rest - turns * 7.549789948768648e-08
    square = rest * rest
    sine = ((-1.9515295891e-4 * square + 8.3321608736e-3) * square - 1.6666654611e-1) * square
    sine = sine * rest + rest
    cosine = ((2.443315711809948e-5 * square - 1.388731625493765e-3) * square + 4.166664568298827e-2)
    cosine = cosine * square * square - 0.5 * square + 1.0
    quarter = turns.astype(jnp.int32) & 3
    swap = (quarter & 1) == 1
    sine_out = jnp.where(swap, cosine, sine)
    cosine_out = jnp.where(swap, sine, cosine)
    sine_out = jnp.where(quarter >= 2, -sine_out, sine_out)
    cosine_out = jnp.where((quarter == 1) | (quarter == 2), -cosine_out, cosine_out)
    return sine_out, cosine_out


def stacked(left, right):
    rows = left.shape[0]
    high, low = halves(left)
    both = jnp.dot(jnp.concatenate([high, low], axis=0), right[0], preferred_element_type=F32)
    out = both[:rows] + both[rows:]
    if right[1] is None:
        return out
    return out + jnp.dot(high, right[1], preferred_element_type=F32)


def goldstein_looks(padded, tables):
    left_both = jnp.concatenate([tables[0][...], tables[1][...]], axis=0)
    back_both = jnp.concatenate([tables[4][...], tables[5][...]], axis=0)
    right = (tables[2], tables[3])
    back_right = (tables[6], tables[7])
    band, same = tables[8][...], tables[9][...]
    step, wide = PATCH // 2, 4 * PATCH
    lines, samples = padded.shape[1:]
    block_rows = (lines - step) // step
    groups = (samples - LANES) // LANES

    def table_first(both, value):
        rows = both.shape[0] // 2
        high, low = halves(value)
        first = jnp.dot(both, high, preferred_element_type=F32)
        return first[:rows] + first[rows:] + jnp.dot(both[:rows], low, preferred_element_type=F32)

    columns = []
    for u in range(block_rows):
        strip = jnp.concatenate(
            [padded[0, u * step : u * step + PATCH], padded[1, u * step : u * step + PATCH]], axis=0
        )
        columns.append(table_first(left_both, strip))
    windows = [slice(q * LANES, q * LANES + wide) for q in range(groups)]
    real = jnp.concatenate([c[:PATCH, w] for w in windows for c in columns], axis=0)
    imag = jnp.concatenate([c[PATCH:, w] for w in windows for c in columns], axis=0)
    spectrum = stacked(real, (right[0][:wide], right[1][:wide])) + stacked(
        imag, (right[0][wide:], right[1][wide:])
    )
    spec_re, spec_im = spectrum[:, :wide], spectrum[:, wide:]
    size = jnp.sqrt(spec_re * spec_re + spec_im * spec_im)
    across = stacked(size, (band, None))
    patches = groups * block_rows
    pieces = [slice(p * PATCH, (p + 1) * PATCH) for p in range(patches)]
    column_sums = jnp.concatenate(
        [jnp.sum(size[p], axis=0, keepdims=True) for p in pieces], axis=0
    )
    if patches % 16:
        column_sums = jnp.concatenate(
            [column_sums, jnp.zeros((16 - patches % 16, wide), F32)], axis=0
        )
    total = stacked(column_sums, (same, None))
    scale = (1.0 / 9.0) / (total * (1.0 / PATCH**2) + EPS)
    gains = []
    for p, piece in enumerate(pieces):
        part = across[piece]
        around = part + pltpu.roll(part, 1, 0) + pltpu.roll(part, PATCH - 1, 0)
        gains.append(jnp.sqrt(around * scale[p : p + 1]))
    gain = jnp.concatenate(gains, axis=0)
    rows = stacked(spec_re * gain, (back_right[0][:wide], back_right[1][:wide])) + stacked(
        spec_im * gain, (back_right[0][wide:], back_right[1][wide:])
    )
    half = rows.shape[1] // 2
    looks = []
    for u in range(block_rows):
        parts = [rows[pieces[q * block_rows + u]] for q in range(groups)]
        value = jnp.concatenate(
            [
                jnp.concatenate([x[:, :half] for x in parts], axis=1),
                jnp.concatenate([x[:, half:] for x in parts], axis=1),
            ],
            axis=0,
        )
        looks.append(table_first(back_both, value))
    half = looks[0].shape[0] // 2
    return [jnp.concatenate([x[:half] for x in looks], axis=0), jnp.concatenate([x[half:] for x in looks], axis=0)]


def anchors(owner, base, tile_lat, tile_lon, count_rg):
    row = owner // count_rg * tile_lat + base // tile_lon
    return row, owner % count_rg * tile_lon + base % tile_lon


def place_rows(anchor_row, share_ref, row_ref):
    row_ids = lax.broadcasted_iota(jnp.int32, (row_ref.shape[1], LANES), 0)
    for i in range(anchor_row.shape[0]):
        span = slice(i * LANES, (i + 1) * LANES)
        gap = row_ids - anchor_row[i : i + 1]
        for c in range(2):
            upper, lower = share_ref[c : c + 1, span], share_ref[2 + c : 3 + c, span]
            row_ref[c, :, span] = jnp.where(gap == 0, upper, jnp.where(gap == 1, lower, 0.0))


def place_columns(anchor_col, hit_ref):
    col_ids = lax.broadcasted_iota(jnp.int32, (LANES, hit_ref.shape[1]), 1).astype(F32)
    for i in range(anchor_col.shape[0]):
        column = jnp.broadcast_to(anchor_col[i : i + 1].astype(F32), (LANES, LANES)).T
        column = jnp.concatenate([column] * (hit_ref.shape[1] // LANES), axis=1)
        hit_ref[i * LANES : (i + 1) * LANES, :] = jnp.where(column == col_ids, 1.0, 0.0).astype(BF16)


def splat(row_ref, hit_ref, look):
    chunks = hit_ref.shape[0] // LANES
    rows = row_ref.shape[1]
    values = []
    for c in range(2):
        if look is None:
            value = row_ref[c]
        else:
            value = jnp.concatenate(
                [row_ref[c, :, i * LANES : (i + 1) * LANES] * look[i : i + 1] for i in range(chunks)],
                axis=1,
            )
        values += halves(value)
    sums = jnp.dot(jnp.concatenate(values, axis=0), hit_ref[...], preferred_element_type=F32)
    moved = pltpu.roll(sums[2 * rows : 3 * rows] + sums[3 * rows :], 1, 1)
    first = lax.broadcasted_iota(jnp.int32, moved.shape, 1) == 0
    return sums[:rows] + sums[rows : 2 * rows] + jnp.where(first, 0.0, moved)


MESH = pl.DeviceIdType.MESH


def peers(count_az):
    az, rg = lax.axis_index("az"), lax.axis_index("rg")
    others = [{"az": lax.rem(az + d, count_az), "rg": rg} for d in range(1, count_az)]
    return az, rg, others, {"az": az, "rg": 1 - rg}


def greet(devices):
    barrier = pltpu.get_barrier_semaphore()
    for device in devices:
        pl.semaphore_signal(barrier, inc=1, device_id=device, device_id_type=MESH)
    pl.semaphore_wait(barrier, len(devices))


def remote(source, target, send_sem, recv_sem, device):
    return pltpu.make_async_remote_copy(
        src_ref=source,
        dst_ref=target,
        send_sem=send_sem,
        recv_sem=recv_sem,
        device_id=device,
        device_id_type=MESH,
    )


def look_up(table_ref, heights_ref, lane_ref, row_ref, lines, rows, fresh):
    count = lines.stop - lines.start

    def one_column(column, carry):
        span = pl.ds(pl.multiple_of(column * LANES, LANES), LANES)
        lane, row = lane_ref[lines, span], row_ref[lines, span]
        heights = jnp.zeros((count, LANES), F32) if fresh else heights_ref[lines, span]
        for r in rows:
            source = jnp.broadcast_to(table_ref[r // 8, r % 8 : r % 8 + 1, :], (count, LANES))
            picked = jnp.take_along_axis(source, lane, axis=1, mode="promise_in_bounds")
            heights = jnp.where(row == r, picked, heights)
        heights_ref[lines, span] = heights
        return carry

    lax.fori_loop(0, heights_ref.shape[1] // LANES, one_column, 0)


def flatten_lines(image_ref, factor_ref, heights_ref, flat_ref, lines):
    sine, cosine = sine_cosine(factor_ref[lines, :] * heights_ref[lines, :])
    real, imag = image_ref[0, lines, :], image_ref[1, lines, :]
    flat_ref[0, lines, :] = real * cosine + imag * sine
    flat_ref[1, lines, :] = imag * cosine - real * sine


def whole_kernel(
    count_az,
    rim,
    slot_groups,
    *refs,
):
    sources, refs = refs[:18], refs[18:]
    out_ref, refs = refs[0], refs[1:]
    held, refs = refs[:18], refs[18:]
    list_ref, terrain_ref, position_ref, owner_ref, base_ref, share_ref, factor_ref, image_ref = held[:8]
    tables = held[8:]
    (
        load_sems,
        extended,
        edge,
        own_list,
        lists,
        lists_smem,
        outgoing,
        incoming,
        table_ref,
        heights_ref,
        lane_ref,
        row_ref,
        flat_ref,
        top,
        bottom,
        side,
        top_side,
        bottom_side,
        edge_sems,
        list_send,
        list_recv,
        block_send,
        block_recv,
        local_sem,
        send,
        recv,
        padded_ref,
        weight_ref,
        hit_ref,
        sums_ref,
        half,
        near,
        far,
        near_send,
        near_recv,
        far_send,
        far_recv,
    ) = refs
    north, east = terrain_ref.shape[:2]
    slots = list_ref.shape[1]
    block = extended.shape[1:]
    lines, samples = factor_ref.shape
    az, rg, others, partner = peers(count_az)
    barrier = pltpu.get_barrier_semaphore()
    crossed = [
        {"az": lax.rem(az + d, count_az), "rg": 1 - rg} for d in (1, count_az - 1)
    ]
    greeted = others + [partner] + crossed
    for device in greeted:
        pl.semaphore_signal(barrier, inc=1, device_id=device, device_id_type=MESH)
    loads = [
        pltpu.make_async_copy(source, target, load_sems.at[n])
        for n, (source, target) in enumerate(zip(sources, held))
    ]
    for load in loads:
        load.start()
    loads[0].wait()
    own_list[...] = jnp.full(own_list.shape, -1, jnp.int32)
    own_list[0:1, 0:slots] = list_ref[...]
    lists[0] = own_list[...]
    loads[1].wait()
    for lat in range(north):
        extended[lat * east : (lat + 1) * east] = terrain_ref[lat].reshape((east,) + block)
    extended[north * east + north] = jnp.zeros(block, F32)
    for lat in range(north):
        edge[lat] = jnp.where(rg == 0, extended[lat * east + east - 1], extended[lat * east])
    pl.semaphore_wait(barrier, len(greeted))
    list_copies = [
        remote(own_list, lists.at[d + 1], list_send.at[d], list_recv.at[d], device)
        for d, device in enumerate(others)
    ]
    for copy in list_copies:
        copy.start()
    edge_copy = remote(
        edge, extended.at[pl.ds(north * east, north)], edge_sems.at[0], edge_sems.at[1], partner
    )
    edge_copy.start()
    channels, map_lat, map_lon = sums_ref.shape
    tile, lanes = out_ref.shape[1:]
    mine = pl.ds(pl.multiple_of(rg * lanes, LANES), lanes)
    theirs = pl.ds(pl.multiple_of((1 - rg) * lanes, LANES), lanes)
    near_copies = [
        remote(sums_ref.at[c, :, theirs], near.at[c], near_send.at[c], near_recv.at[c], partner)
        for c in range(channels)
    ]
    far_copies = [
        [
            remote(
                half.at[c, pl.ds(pl.multiple_of(device["az"] * tile, 8), tile), :],
                far.at[c, d],
                far_send.at[c, d],
                far_recv.at[c, d],
                device,
            )
            for d, device in enumerate(others)
        ]
        for c in range(channels)
    ]

    def spread(c):
        near_copies[c].wait()
        half[c] = sums_ref[c, :, mine] + near[c]
        for copy in far_copies[c]:
            copy.start()

    def gathered(c):
        total = half[c, pl.ds(pl.multiple_of(az * tile, 8), tile), :]
        for d, copy in enumerate(far_copies[c]):
            copy.wait()
            total = total + far[c, d]
        return total

    loads[2].wait()
    position = position_ref[...]
    lane_ref[...] = position & (LANES - 1)
    row_ref[...] = lax.shift_right_logical(position, LANES.bit_length() - 1)
    for n in range(3, 6):
        loads[n].wait()
    anchor_row, anchor_col = anchors(owner_ref[...], base_ref[...], tile, lanes, map_lon // lanes)
    place_rows(anchor_row, share_ref, weight_ref)
    for copy in list_copies:
        copy.wait()
    to_smem = pltpu.make_async_copy(lists, lists_smem, local_sem)
    to_smem.start()
    edge_copy.wait()
    to_smem.wait()

    def pick(d, slot):
        number = lists_smem[d, 0, slot]
        lat = number // (2 * east) - az * north
        lon = number % (2 * east) - rg * east
        inside = (number >= 0) & (lat >= 0) & (lat < north)
        at_edge = (lon < 0) | (lon >= east)
        place = jnp.where(at_edge, north * east + lat, lat * east + lon)
        return extended[jnp.where(inside, place, north * east + north)]

    copies = []
    for g, group in enumerate(slot_groups):
        span = pl.ds(group.start, len(group))
        for d in range(1, count_az):
            for slot in group:
                outgoing[d - 1, slot] = pick(d, slot)
            device = {"az": lax.rem(az + count_az - d, count_az), "rg": rg}
            copy = remote(
                outgoing.at[d - 1, span],
                incoming.at[d - 1, span],
                block_send.at[g, d - 1],
                block_recv.at[g, d - 1],
                device,
            )
            copy.start()
            copies.append(copy)
    for slot in range(slots):
        table_ref[slot] = pick(0, slot)
    place_columns(anchor_col, hit_ref)
    sums_ref[2] = splat(weight_ref, hit_ref, None)
    near_copies[2].start()
    for load in loads[6:]:
        load.wait()
    first, middle, last = slice(0, rim), slice(rim, lines - rim), slice(lines - rim, lines)
    for g, group in enumerate(slot_groups):
        span = slice(group.start, group.stop)
        total = table_ref[span]
        for d in range(count_az - 1):
            copies[g * (count_az - 1) + d].wait()
            total = total + incoming[d, span]
        table_ref[span] = total
        rows = range(group.start * block[0], group.stop * block[0])
        if g < len(slot_groups) - 1:
            look_up(table_ref, heights_ref, lane_ref, row_ref, slice(0, lines), rows, g == 0)
        else:
            look_up(table_ref, heights_ref, lane_ref, row_ref, first, rows, g == 0)
            look_up(table_ref, heights_ref, lane_ref, row_ref, last, rows, g == 0)
    for part in (first, last):
        flatten_lines(image_ref, factor_ref, heights_ref, flat_ref, part)
    beside = pl.ds(pl.multiple_of((1 - rg) * (samples - LANES), LANES), LANES)
    first_ds, last_ds = pl.ds(0, rim), pl.ds(lines - rim, rim)
    above, below = az - 1, az + 1
    up = [
        remote(flat_ref.at[:, first_ds, :], bottom, send.at[1], recv.at[2], {"az": above, "rg": rg}),
        remote(
            flat_ref.at[:, first_ds, beside], bottom_side, send.at[2], recv.at[4], {"az": above, "rg": 1 - rg}
        ),
    ]
    down = [
        remote(flat_ref.at[:, last_ds, :], top, send.at[3], recv.at[1], {"az": below, "rg": rg}),
        remote(
            flat_ref.at[:, last_ds, beside], top_side, send.at[4], recv.at[3], {"az": below, "rg": 1 - rg}
        ),
    ]

    @pl.when(az > 0)
    def _():
        for copy in up:
            copy.start()

    @pl.when(az < count_az - 1)
    def _():
        for copy in down:
            copy.start()

    look_up(table_ref, heights_ref, lane_ref, row_ref, middle, rows, len(slot_groups) == 1)
    flatten_lines(image_ref, factor_ref, heights_ref, flat_ref, middle)
    side_copy = remote(flat_ref.at[:, :, beside], side, send.at[0], recv.at[0], partner)
    side_copy.start()

    def place(target, centre, nearby):
        left = jnp.where(rg == 1, nearby, 0.0)
        right = jnp.where(rg == 0, nearby, 0.0)
        for part in range(2):
            wide = jnp.concatenate([left[part], centre[part], right[part]], axis=1)
            padded_ref[part, target, :] = wide[:, LANES - rim : 2 * LANES - rim + samples]

    side_copy.wait()
    place(slice(rim, rim + lines), flat_ref[...], side[...])

    @pl.when(az > 0)
    def _():
        for copy in up:
            copy.wait_send()

    @pl.when(az < count_az - 1)
    def _():
        for copy in down:
            copy.wait_send()

    @pl.when(az > 0)
    def _():
        for copy in down:
            copy.wait_recv()
        place(slice(0, rim), top[...], top_side[...])

    @pl.when(az == 0)
    def _():
        padded_ref[:, :rim, :] = jnp.zeros((2, rim, padded_ref.shape[2]), F32)

    @pl.when(az < count_az - 1)
    def _():
        for copy in up:
            copy.wait_recv()
        place(slice(rim + lines, 2 * rim + lines), bottom[...], bottom_side[...])

    @pl.when(az == count_az - 1)
    def _():
        padded_ref[:, rim + lines :, :] = jnp.zeros((2, rim, padded_ref.shape[2]), F32)

    spread(2)
    looks = goldstein_looks(padded_ref, tables)
    sums_ref[0] = splat(weight_ref, hit_ref, looks[0])
    near_copies[0].start()
    sums_ref[1] = splat(weight_ref, hit_ref, looks[1])
    near_copies[1].start()
    spread(0)
    spread(1)
    weight = jnp.maximum(gathered(2), 1.0)
    out_ref[0] = gathered(0) / weight
    out_ref[1] = gathered(1) / weight


def body(
    complex_phase_image,
    phase_to_topography_factor,
    terrain_model_heights,
    radar_parcel_listing,
    pixel_terrain_position,
    multilook_receiving_patch,
    multilook_base_point,
    multilook_splat_shares,
):
    count_az = lax.axis_size("az")
    count_rg = lax.axis_size("rg")
    assert count_rg == 2
    north, east, points = terrain_model_heights.shape
    slots = radar_parcel_listing.shape[1]
    az_lines, rg_samples = phase_to_topography_factor.shape
    dma = pltpu.SemaphoreType.DMA
    block = (points // LANES, LANES)
    rim = PATCH // 4
    groups = [range(start, min(start + 3, slots)) for start in range(0, slots, 3)]
    tile = (az_lines, rg_samples)
    map_lat = az_lines // LOOK
    map_lon = rg_samples // LOOK
    chunks = map_lat * map_lon // LANES
    whole_lat, whole_lon = map_lat * count_az, map_lon * count_rg
    operands = [
        radar_parcel_listing,
        terrain_model_heights,
        pixel_terrain_position,
        multilook_receiving_patch.reshape(chunks, LANES),
        multilook_base_point.reshape(chunks, LANES),
        multilook_splat_shares,
        phase_to_topography_factor,
        complex_phase_image,
    ] + [jnp.asarray(table) for table in filter_tables()]
    assert len(operands) == 18
    return pl.pallas_call(
        functools.partial(whole_kernel, count_az, rim, groups),
        out_shape=jax.ShapeDtypeStruct((2, map_lat, map_lon), F32),
        in_specs=[pl.BlockSpec(memory_space=pl.ANY)] * len(operands),
        scratch_shapes=[pltpu.VMEM(x.shape, x.dtype) for x in operands]
        + [
            dma((len(operands),)),
            pltpu.VMEM((north * east + north + 1,) + block, F32),
            pltpu.VMEM((north,) + block, F32),
            pltpu.VMEM((8, LANES), jnp.int32),
            pltpu.VMEM((count_az, 8, LANES), jnp.int32),
            pltpu.SMEM((count_az, 8, LANES), jnp.int32),
            pltpu.VMEM((count_az - 1, slots) + block, F32),
            pltpu.VMEM((count_az - 1, slots) + block, F32),
            pltpu.VMEM((slots,) + block, F32),
            pltpu.VMEM(tile, F32),
            pltpu.VMEM(tile, jnp.int32),
            pltpu.VMEM(tile, jnp.int32),
            pltpu.VMEM((2,) + tile, F32),
            pltpu.VMEM((2, rim, rg_samples), F32),
            pltpu.VMEM((2, rim, rg_samples), F32),
            pltpu.VMEM((2, az_lines, LANES), F32),
            pltpu.VMEM((2, rim, LANES), F32),
            pltpu.VMEM((2, rim, LANES), F32),
            dma((2,)),
            dma((count_az - 1,)),
            dma((count_az - 1,)),
            dma((len(groups), count_az - 1)),
            dma((len(groups), count_az - 1)),
            dma,
            dma((5,)),
            dma((5,)),
            pltpu.VMEM((2, az_lines + 2 * rim, rg_samples + LANES), F32),
            pltpu.VMEM((2, whole_lat, chunks * LANES), F32),
            pltpu.VMEM((chunks * LANES, whole_lon), BF16),
            pltpu.VMEM((3, whole_lat, whole_lon), F32),
            pltpu.VMEM((3, whole_lat, map_lon), F32),
            pltpu.VMEM((3, whole_lat, map_lon), F32),
            pltpu.VMEM((3, count_az - 1, map_lat, map_lon), F32),
            dma((3,)),
            dma((3,)),
            dma((3, count_az - 1)),
            dma((3, count_az - 1)),
        ],
        compiler_params=pltpu.CompilerParams(
            collective_id=0, has_side_effects=True, vmem_limit_bytes=56 * 1024 * 1024
        ),
        name="interferogram_map",
    )(*operands)


def solution(mesh):
    return jax.shard_map(
        body,
        mesh=mesh,
        in_specs=(
            P(None, ("scene", "az"), "rg"),
            P(("scene", "az"), "rg"),
            P(("scene", "az"), "rg", None),
            P(("scene", "az", "rg"), None),
            P(("scene", "az"), "rg"),
            P(("scene", "az", "rg"), None),
            P(("scene", "az", "rg")),
            P(None, ("scene", "az", "rg")),
        ),
        out_specs=P(None, ("scene", "az"), "rg"),
        check_vma=False,
    )
```

profile of v0, /device:TPU:0, one launch (start us, length us, event | category | flops | bytes accessed | tf_op | source)
XLA Modules:
  0.0 40.6 jit_solution(12378061774687756556)
XLA Ops:
  0.0 39.3 %interferogram_map.1 = f32[2,16,128]{2,1,0:T(8,128)} custom-call(s32[1,9]{1,0:T(1,128)} %refs_0_.1, f32[8,8,1024]{2,1,0:T(8,128)} %refs_1_.1, s32[64,512]{1,0:T(8,128)} %refs_2_.1, s32[16,128]{1,0:T(8,128)} %bitcast.2, s32[16,128]{1,0:T(8,128)} %bitcast.3, f32[4,2048]{1,0:T(4,128)} %refs_5_.1, f32[64,512]{1,0:T(8,128)} %refs_6_.1, f32[2,64,512]{2,1,0:T(8,128)} %refs_7_.1, ...), custom_call_target="tpu_custom_call" | custom-call | tf_op jit(solution)/shard_map/interferogram_map/pallas_call | solution.py:564
  39.3 1.3 %copy.20 = f32[2,16,128]{2,1,0:T(8,128)} copy(f32[2,16,128]{2,1,0:T(8,128)} %interferogram_map.1) | data formatting | bytes 32768
where the time goes:
time: 40.9 us; the launch traced here: 40.6 us
  Pallas kernels  39.3 us (96%)
  local copies, waits for them, and re-layouts  1.32 us (3%)
    pallas_call x1, Pallas kernels, body(): pl.pallas_call(functools.partial(whole_kernel, count_az, rim, groups), ou...  39.3 us
    unnamed x1, local copies, waits for them, and re-layouts  1.32 us

commit v1 on v0

--- a/solution.py
+++ b/solution.py
@@ -230,18 +230,29 @@
     )
 
 
-def look_up(table_ref, heights_ref, lane_ref, row_ref, lines, rows, fresh):
-    count = lines.stop - lines.start
-
+def spread_rows(table_ref, wide_ref, rows):
+    for r in rows:
+        wide_ref[r] = jnp.broadcast_to(table_ref[r // 8, r % 8 : r % 8 + 1, :], wide_ref.shape[1:])
+
+
+def look_up(wide_ref, heights_ref, lane_ref, row_ref, pieces, rows, fresh):
     def one_column(column, carry):
         span = pl.ds(pl.multiple_of(column * LANES, LANES), LANES)
-        lane, row = lane_ref[lines, span], row_ref[lines, span]
-        heights = jnp.zeros((count, LANES), F32) if fresh else heights_ref[lines, span]
+        lane = jnp.concatenate([lane_ref[piece, span] for piece in pieces], axis=0)
+        row = jnp.concatenate([row_ref[piece, span] for piece in pieces], axis=0)
+        if fresh:
+            heights = jnp.zeros(lane.shape, F32)
+        else:
+            heights = jnp.concatenate([heights_ref[piece, span] for piece in pieces], axis=0)
         for r in rows:
-            source = jnp.broadcast_to(table_ref[r // 8, r % 8 : r % 8 + 1, :], (count, LANES))
+            source = jnp.concatenate([wide_ref[r]] * (lane.shape[0] // wide_ref.shape[1]), axis=0)
             picked = jnp.take_along_axis(source, lane, axis=1, mode="promise_in_bounds")
             heights = jnp.where(row == r, picked, heights)
-        heights_ref[lines, span] = heights
+        start = 0
+        for piece in pieces:
+            count = piece.stop - piece.start
+            heights_ref[piece, span] = heights[start : start + count]
+            start += count
         return carry
 
     lax.fori_loop(0, heights_ref.shape[1] // LANES, one_column, 0)
@@ -275,6 +286,7 @@
         outgoing,
         incoming,
         table_ref,
+        wide_ref,
         heights_ref,
         lane_ref,
         row_ref,
@@ -314,13 +326,15 @@
         {"az": lax.rem(az + d, count_az), "rg": 1 - rg} for d in (1, count_az - 1)
     ]
     greeted = others + [partner] + crossed
-    for device in greeted:
-        pl.semaphore_signal(barrier, inc=1, device_id=device, device_id_type=MESH)
     loads = [
         pltpu.make_async_copy(source, target, load_sems.at[n])
         for n, (source, target) in enumerate(zip(sources, held))
     ]
-    for load in loads:
+    for load in loads[:2]:
+        load.start()
+    for device in greeted:
+        pl.semaphore_signal(barrier, inc=1, device_id=device, device_id_type=MESH)
+    for load in loads[2:8]:
         load.start()
     loads[0].wait()
     own_list[...] = jnp.full(own_list.shape, -1, jnp.int32)
@@ -343,6 +357,8 @@
         edge, extended.at[pl.ds(north * east, north)], edge_sems.at[0], edge_sems.at[1], partner
     )
     edge_copy.start()
+    for load in loads[8:]:
+        load.start()
     channels, map_lat, map_lon = sums_ref.shape
     tile, lanes = out_ref.shape[1:]
     mine = pl.ds(pl.multiple_of(rg * lanes, LANES), lanes)
@@ -434,11 +450,8 @@
             total = total + incoming[d, span]
         table_ref[span] = total
         rows = range(group.start * block[0], group.stop * block[0])
-        if g < len(slot_groups) - 1:
-            look_up(table_ref, heights_ref, lane_ref, row_ref, slice(0, lines), rows, g == 0)
-        else:
-            look_up(table_ref, heights_ref, lane_ref, row_ref, first, rows, g == 0)
-            look_up(table_ref, heights_ref, lane_ref, row_ref, last, rows, g == 0)
+        spread_rows(table_ref, wide_ref, rows)
+        look_up(wide_ref, heights_ref, lane_ref, row_ref, (first, last), rows, g == 0)
     for part in (first, last):
         flatten_lines(image_ref, factor_ref, heights_ref, flat_ref, part)
     beside = pl.ds(pl.multiple_of((1 - rg) * (samples - LANES), LANES), LANES)
@@ -467,7 +480,7 @@
         for copy in down:
             copy.start()
 
-    look_up(table_ref, heights_ref, lane_ref, row_ref, middle, rows, len(slot_groups) == 1)
+    look_up(wide_ref, heights_ref, lane_ref, row_ref, (middle,), range(slots * block[0]), True)
     flatten_lines(image_ref, factor_ref, heights_ref, flat_ref, middle)
     side_copy = remote(flat_ref.at[:, :, beside], side, send.at[0], recv.at[0], partner)
     side_copy.start()
@@ -576,6 +589,7 @@
             pltpu.VMEM((count_az - 1, slots) + block, F32),
             pltpu.VMEM((count_az - 1, slots) + block, F32),
             pltpu.VMEM((slots,) + block, F32),
+            pltpu.VMEM((slots * block[0], 8, LANES), F32),
             pltpu.VMEM(tile, F32),
             pltpu.VMEM(tile, jnp.int32),
             pltpu.VMEM(tile, jnp.int32),

time: 40.9 us -> 40.7 us (level)
  no operation moved by 1% of the time
where the time goes in v1:
time: 40.7 us; the launch traced here: 40.4 us
  Pallas kernels  39.1 us (96%)
  local copies, waits for them, and re-layouts  1.32 us (3%)
    pallas_call x1, Pallas kernels, body(): pl.pallas_call(functools.partial(whole_kernel, count_az, rim, groups), ou...  39.1 us
    unnamed x1, local copies, waits for them, and re-layouts  1.32 us

profile of v1, /device:TPU:0, one launch (start us, length us, event | category | flops | bytes accessed | tf_op | source)
XLA Modules:
  0.0 40.4 jit_solution(5276318422042260836)
XLA Ops:
  0.0 39.1 %interferogram_map.1 = f32[2,16,128]{2,1,0:T(8,128)} custom-call(s32[1,9]{1,0:T(1,128)} %refs_0_.1, f32[8,8,1024]{2,1,0:T(8,128)} %refs_1_.1, s32[64,512]{1,0:T(8,128)} %refs_2_.1, s32[16,128]{1,0:T(8,128)} %bitcast.2, s32[16,128]{1,0:T(8,128)} %bitcast.3, f32[4,2048]{1,0:T(4,128)} %refs_5_.1, f32[64,512]{1,0:T(8,128)} %refs_6_.1, f32[2,64,512]{2,1,0:T(8,128)} %refs_7_.1, ...), custom_call_target="tpu_custom_call" | custom-call | tf_op jit(solution)/shard_map/interferogram_map/pallas_call | solution.py:577
  39.1 1.3 %copy.20 = f32[2,16,128]{2,1,0:T(8,128)} copy(f32[2,16,128]{2,1,0:T(8,128)} %interferogram_map.1) | data formatting | bytes 32768

commit v2 on v1

--- a/solution.py
+++ b/solution.py
@@ -235,8 +235,12 @@
         wide_ref[r] = jnp.broadcast_to(table_ref[r // 8, r % 8 : r % 8 + 1, :], wide_ref.shape[1:])
 
 
-def look_up(wide_ref, heights_ref, lane_ref, row_ref, pieces, rows, fresh):
-    def one_column(column, carry):
+def look_up(wide_ref, heights_ref, lane_ref, row_ref, pieces, rows, fresh, columns, after=None):
+    first, start_at, stop_at = columns
+    count_columns = heights_ref.shape[1] // LANES
+
+    def one_column(step, carry):
+        column = lax.rem(first + step, count_columns)
         span = pl.ds(pl.multiple_of(column * LANES, LANES), LANES)
         lane = jnp.concatenate([lane_ref[piece, span] for piece in pieces], axis=0)
         row = jnp.concatenate([row_ref[piece, span] for piece in pieces], axis=0)
@@ -253,16 +257,18 @@
             count = piece.stop - piece.start
             heights_ref[piece, span] = heights[start : start + count]
             start += count
+        if after is not None:
+            after(span)
         return carry
 
-    lax.fori_loop(0, heights_ref.shape[1] // LANES, one_column, 0)
-
-
-def flatten_lines(image_ref, factor_ref, heights_ref, flat_ref, lines):
-    sine, cosine = sine_cosine(factor_ref[lines, :] * heights_ref[lines, :])
-    real, imag = image_ref[0, lines, :], image_ref[1, lines, :]
-    flat_ref[0, lines, :] = real * cosine + imag * sine
-    flat_ref[1, lines, :] = imag * cosine - real * sine
+    lax.fori_loop(start_at, stop_at, one_column, 0)
+
+
+def flatten_lines(image_ref, factor_ref, heights_ref, flat_ref, lines, span):
+    sine, cosine = sine_cosine(factor_ref[lines, span] * heights_ref[lines, span])
+    real, imag = image_ref[0, lines, span], image_ref[1, lines, span]
+    flat_ref[0, lines, span] = real * cosine + imag * sine
+    flat_ref[1, lines, span] = imag * cosine - real * sine
 
 
 def whole_kernel(
@@ -451,9 +457,11 @@
         table_ref[span] = total
         rows = range(group.start * block[0], group.stop * block[0])
         spread_rows(table_ref, wide_ref, rows)
-        look_up(wide_ref, heights_ref, lane_ref, row_ref, (first, last), rows, g == 0)
+        look_up(
+            wide_ref, heights_ref, lane_ref, row_ref, (first, last), rows, g == 0, (0, 0, samples // LANES)
+        )
     for part in (first, last):
-        flatten_lines(image_ref, factor_ref, heights_ref, flat_ref, part)
+        flatten_lines(image_ref, factor_ref, heights_ref, flat_ref, part, slice(None))
     beside = pl.ds(pl.multiple_of((1 - rg) * (samples - LANES), LANES), LANES)
     first_ds, last_ds = pl.ds(0, rim), pl.ds(lines - rim, rim)
     above, below = az - 1, az + 1
@@ -480,10 +488,23 @@
         for copy in down:
             copy.start()
 
-    look_up(wide_ref, heights_ref, lane_ref, row_ref, (middle,), range(slots * block[0]), True)
-    flatten_lines(image_ref, factor_ref, heights_ref, flat_ref, middle)
+    def middle_part(start_at, stop_at):
+        look_up(
+            wide_ref,
+            heights_ref,
+            lane_ref,
+            row_ref,
+            (middle,),
+            range(slots * block[0]),
+            True,
+            ((1 - rg) * (samples // LANES - 1), start_at, stop_at),
+            lambda span: flatten_lines(image_ref, factor_ref, heights_ref, flat_ref, middle, span),
+        )
+
+    middle_part(0, 1)
     side_copy = remote(flat_ref.at[:, :, beside], side, send.at[0], recv.at[0], partner)
     side_copy.start()
+    middle_part(1, samples // LANES)
 
     def place(target, centre, nearby):
         left = jnp.where(rg == 1, nearby, 0.0)
@@ -557,7 +578,8 @@
     dma = pltpu.SemaphoreType.DMA
     block = (points // LANES, LANES)
     rim = PATCH // 4
-    groups = [range(start, min(start + 3, slots)) for start in range(0, slots, 3)]
+    cuts = sorted({0, 4 * slots // 9, 7 * slots // 9, slots})
+    groups = [range(start, stop) for start, stop in zip(cuts, cuts[1:])]
     tile = (az_lines, rg_samples)
     map_lat = az_lines // LOOK
     map_lon = rg_samples // LOOK
@@ -576,7 +598,7 @@
     assert len(operands) == 18
     return pl.pallas_call(
         functools.partial(whole_kernel, count_az, rim, groups),
-        out_shape=jax.ShapeDtypeStruct((2, map_lat, map_lon), F32),
+        out_shape=pltpu.VMEM((2, map_lat, map_lon), F32),
         in_specs=[pl.BlockSpec(memory_space=pl.ANY)] * len(operands),
         scratch_shapes=[pltpu.VMEM(x.shape, x.dtype) for x in operands]
         + [

time: 40.7 us -> 38.4 us (0.943)
  Pallas kernels: 39.1 us -> 37.7 us
  local copies, waits for them, and re-layouts: 1.32 us -> 0.61 us
    pallas_call x1, Pallas kernels: 39.1 us -> 37.7 us  [body(): pl.pallas_call(functools.partial(whole_kernel, count_az, rim, groups), ou...]
    unnamed x1, local copies, waits for them, and re-layouts: 1.32 us -> 0.61 us
where the time goes in v2:
time: 38.4 us; the launch traced here: 38.3 us
  Pallas kernels  37.7 us (98%)
  local copies, waits for them, and re-layouts  0.61 us (2%)
    pallas_call x1, Pallas kernels, body(): pl.pallas_call(functools.partial(whole_kernel, count_az, rim, groups), ou...  37.7 us

profile of v2, /device:TPU:0, one launch (start us, length us, event | category | flops | bytes accessed | tf_op | source)
XLA Modules:
  0.0 38.3 jit_solution(2133013627020364091)
XLA Ops:
  0.0 37.7 %interferogram_map.1 = f32[2,16,128]{2,1,0:T(8,128)S(1)} custom-call(s32[1,9]{1,0:T(1,128)} %refs_0_.1, f32[8,8,1024]{2,1,0:T(8,128)} %refs_1_.1, s32[64,512]{1,0:T(8,128)} %refs_2_.1, s32[16,128]{1,0:T(8,128)} %bitcast.2, s32[16,128]{1,0:T(8,128)} %bitcast.3, f32[4,2048]{1,0:T(4,128)} %refs_5_.1, f32[64,512]{1,0:T(8,128)} %refs_6_.1, ...), custom_call_target="tpu_custom_call" | custom-call | tf_op jit(solution)/shard_map/interferogram_map/pallas_call | solution.py:599
  37.7 0.6 %copy.20 = f32[2,16,128]{2,1,0:T(8,128)} copy(f32[2,16,128]{2,1,0:T(8,128)S(1)} %interferogram_map.1) | data formatting | bytes 32768

commit v3 on v2

--- a/solution.py
+++ b/solution.py
@@ -346,12 +346,6 @@
     own_list[...] = jnp.full(own_list.shape, -1, jnp.int32)
     own_list[0:1, 0:slots] = list_ref[...]
     lists[0] = own_list[...]
-    loads[1].wait()
-    for lat in range(north):
-        extended[lat * east : (lat + 1) * east] = terrain_ref[lat].reshape((east,) + block)
-    extended[north * east + north] = jnp.zeros(block, F32)
-    for lat in range(north):
-        edge[lat] = jnp.where(rg == 0, extended[lat * east + east - 1], extended[lat * east])
     pl.semaphore_wait(barrier, len(greeted))
     list_copies = [
         remote(own_list, lists.at[d + 1], list_send.at[d], list_recv.at[d], device)
@@ -359,6 +353,12 @@
     ]
     for copy in list_copies:
         copy.start()
+    loads[1].wait()
+    for lat in range(north):
+        extended[lat * east : (lat + 1) * east] = terrain_ref[lat].reshape((east,) + block)
+    extended[north * east + north] = jnp.zeros(block, F32)
+    for lat in range(north):
+        edge[lat] = jnp.where(rg == 0, extended[lat * east + east - 1], extended[lat * east])
     edge_copy = remote(
         edge, extended.at[pl.ds(north * east, north)], edge_sems.at[0], edge_sems.at[1], partner
     )
@@ -417,8 +417,8 @@
 
     def pick(d, slot):
         number = lists_smem[d, 0, slot]
-        lat = number // (2 * east) - az * north
-        lon = number % (2 * east) - rg * east
+        lat = lax.div(number, 2 * east) - az * north
+        lon = lax.rem(number, 2 * east) - rg * east
         inside = (number >= 0) & (lat >= 0) & (lat < north)
         at_edge = (lon < 0) | (lon >= east)
         place = jnp.where(at_edge, north * east + lat, lat * east + lon)
@@ -506,6 +506,8 @@
     side_copy.start()
     middle_part(1, samples // LANES)
 
+    spread(2)
+
     def place(target, centre, nearby):
         left = jnp.where(rg == 1, nearby, 0.0)
         right = jnp.where(rg == 0, nearby, 0.0)
@@ -546,7 +548,6 @@
     def _():
         padded_ref[:, rim + lines :, :] = jnp.zeros((2, rim, padded_ref.shape[2]), F32)
 
-    spread(2)
     looks = goldstein_looks(padded_ref, tables)
     sums_ref[0] = splat(weight_ref, hit_ref, looks[0])
     near_copies[0].start()

time: 38.4 us -> 38.4 us (level)
  no operation moved by 1% of the time
where the time goes in v3:
time: 38.4 us; the launch traced here: 38.2 us
  Pallas kernels  37.6 us (98%)
  local copies, waits for them, and re-layouts  0.61 us (2%)
    pallas_call x1, Pallas kernels, body(): pl.pallas_call(functools.partial(whole_kernel, count_az, rim, groups), ou...  37.6 us

profile of v3, /device:TPU:0, one launch (start us, length us, event | category | flops | bytes accessed | tf_op | source)
XLA Modules:
  0.0 38.2 jit_solution(8165394134954119607)
XLA Ops:
  0.0 37.6 %interferogram_map.1 = f32[2,16,128]{2,1,0:T(8,128)S(1)} custom-call(s32[1,9]{1,0:T(1,128)} %refs_0_.1, f32[8,8,1024]{2,1,0:T(8,128)} %refs_1_.1, s32[64,512]{1,0:T(8,128)} %refs_2_.1, s32[16,128]{1,0:T(8,128)} %bitcast.2, s32[16,128]{1,0:T(8,128)} %bitcast.3, f32[4,2048]{1,0:T(4,128)} %refs_5_.1, f32[64,512]{1,0:T(8,128)} %refs_6_.1, ...), custom_call_target="tpu_custom_call" | custom-call | tf_op jit(solution)/shard_map/interferogram_map/pallas_call | solution.py:600
  37.6 0.6 %copy.20 = f32[2,16,128]{2,1,0:T(8,128)} copy(f32[2,16,128]{2,1,0:T(8,128)S(1)} %interferogram_map.1) | data formatting | bytes 32768
